TPU v7x, 32 devices: a whole 2x2x4 slice. The times are simulated.
32 devices in a mesh: sub: 8 (over y, x, core), rep: 4 (over z).
Axes of the slice: x: 2, y: 2, z: 4, core: 2. Of those that a mesh axis runs over, the one named last changes fastest.
Arguments:
- dual_ops: bfloat16 [32, 1024, 1024], P(('sub', 'rep'))
- mode_traces: float32 [32, 6, 1024], P(('sub', 'rep')), may hold values from -0.046875 to 0.046875
- route: int32 [32, 1024], P(('sub', 'rep')), may hold values from 0 to 1023, each once within a row
- mode_block: int32 [32, 1], replicated, may hold values from 0 to 1
- local_gap: float32 [32, 32768], P(None, ('sub', 'rep')), may hold values from -6 to 6
Outputs:
- multipliers: float32 [32, 32768], P(None, ('sub', 'rep'))
- amplitudes: float32 [32, 12], replicated
Inputs may be any that keep to these rules, and one draw needn't show every extreme that they name: Each row of route lists every number below 1024 once. `mode_block`: every aggregate holds at least one subdomain.
All inputs are finite; a program needn't handle non-finite values.
Results may differ from a plain program's by a relative error of at most 0.003.
Values sent between devices are 32-bit elements; how exact they have to be, the bound alone decides.
No kernel may reach another device: no remote copies, remote signals or barrier semaphores. Data moves between devices by JAX's collectives and lax.ppermute only.
A program may use at most 64 MiB of HBM per device.

v0:
```python
import jax
import jax.numpy as jnp
from jax import lax
from jax.experimental import pallas as pl
from jax.experimental.pallas import tpu as pltpu
from jax.sharding import PartitionSpec as P

MODES = 6
AGG_SUBS = 16
ITERS = 2
GROUP = 8
SCALAR_LANES = (MODES, MODES + 1, GROUP + MODES, GROUP + MODES + 1, 2 * GROUP + MODES)

HIGHEST = lax.Precision.HIGHEST
VMEM = pl.BlockSpec(memory_space=pltpu.VMEM)
HBM = pl.BlockSpec(memory_space=pltpu.HBM)
NN = (((1,), (0,)), ((), ()))
NT = (((1,), (1,)), ((), ()))


def split(values):
    high = values.astype(jnp.bfloat16).astype(jnp.float32)
    return jnp.concatenate([high, values - high], axis=0).astype(jnp.bfloat16)


def split_dot(values, matrix, dims):
    rows = values.shape[0]
    both = lax.dot_general(split(values), matrix, dims, preferred_element_type=jnp.float32)
    return both[:rows] + both[rows:]


def small_dot(left, right):
    return jnp.dot(left, right, precision=HIGHEST, preferred_element_type=jnp.float32)


def send_blocks(values, place_ref, near_ref, own_ref, *pair_refs):
    height, per_peer = own_ref.shape
    peers = 2 * len(pair_refs) + 2
    slots = split_dot(values, place_ref[:, : peers * per_peer], NN)
    own_ref[...] = slots[:, :per_peer]
    near_ref[...] = slots[:, per_peer : 2 * per_peer]
    for at, ref in enumerate(pair_refs):
        start = (peers - 2 * at - 2) * per_peer
        ref[:height] = slots[:, start + per_peer : start + 2 * per_peer]
        ref[height:] = slots[:, start : start + per_peer]


def received(near_ref, own_ref, *pair_refs):
    height = own_ref.shape[0]
    got = [near_ref[:height]]
    for at in reversed(range(len(pair_refs))):
        got += [near_ref[(at + 1) * height : (at + 2) * height], pair_refs[at][:height]]
    return jnp.concatenate([*got, own_ref[...]], axis=1)


def spread(values, loads, groups):
    modes = values[loads:]
    label = modes[MODES : MODES + 1]
    used = lax.broadcasted_iota(jnp.int32, modes.shape, 0) < MODES
    parts = [jnp.where(used & (label == group), modes, 0.0) for group in range(groups)]
    return jnp.concatenate([values[:loads], *parts], axis=0)


def by_slot(place_ref):
    rows = place_ref.shape[0]
    return place_ref[:, place_ref.shape[1] - rows :]


def place_kernel(
    route_hbm, block_hbm, gap_hbm, traces_hbm,
    place_ref, values_ref, *refs,
):
    *send_refs, route_ref, block_ref, traces_ref, sems = refs
    loads, rows = gap_hbm.shape
    per_peer = send_refs[0].shape[1]
    peers = rows // per_peer
    copies = [
        pltpu.make_async_copy(source, target, sems.at[at])
        for at, (source, target) in enumerate(
            (
                (route_hbm, route_ref),
                (block_hbm, block_ref),
                (traces_hbm, traces_ref),
                (gap_hbm, values_ref.at[pl.ds(0, loads)]),
            )
        )
    ]
    for copy in copies:
        copy.start()
    own_index = lax.axis_index("sub")
    device = own_index * lax.axis_size("rep") + lax.axis_index("rep")
    row_ids = lax.broadcasted_iota(jnp.int32, (rows, per_peer), 0)
    low = lax.broadcasted_iota(jnp.int32, (per_peer, per_peer), 0)
    high = lax.broadcasted_iota(jnp.int32, (per_peer, per_peer), 1)
    reverse = jnp.where(low + high == per_peer - 1, 1.0, 0.0).astype(jnp.bfloat16)
    copies[0].wait()
    for offset in range(peers):
        start = pl.multiple_of((own_index ^ offset) * per_peer, per_peer)
        hits = row_ids == route_ref[:, pl.ds(start, per_peer)]
        at = (offset if offset else peers) * per_peer
        place_ref[:, at : at + per_peer] = jnp.where(hits, 1.0, 0.0).astype(jnp.bfloat16)
    place_ref[:, :per_peer] = jnp.dot(
        place_ref[:, rows:], reverse, preferred_element_type=jnp.float32
    ).astype(jnp.bfloat16)
    copies[1].wait()
    copies[2].wait()
    blocks = block_ref[...]
    lane = lax.broadcasted_iota(jnp.int32, blocks.shape, 1)
    own_block = jnp.sum(jnp.where(lane == device, blocks, 0), axis=1, keepdims=True)
    modes = traces_ref.shape[0]
    label = jnp.broadcast_to(own_block.astype(jnp.float32), (1, rows))
    for mode in range(modes):
        values_ref[loads + mode : loads + mode + 1] = traces_ref[mode]
    values_ref[loads + modes : loads + modes + 1] = label
    values_ref[loads + modes + 1 :] = jnp.zeros((GROUP - modes - 1, rows), jnp.float32)
    copies[3].wait()
    send_blocks(values_ref[...], place_ref, *send_refs)


def ready_kernel(operator_hbm, place_ref, values_ref, operator_ref, placed_ref, own_ref, image_ref, sem):
    copy = pltpu.make_async_copy(operator_hbm, operator_ref, sem)
    copy.start()
    values = values_ref[...]
    loads = values.shape[0] - GROUP
    own = spread(values, loads, (own_ref.shape[0] - loads) // GROUP)
    own_ref[...] = own
    copy.wait()
    operator = operator_ref[0]
    image_ref[...] = split_dot(own, operator, NT)
    placed_ref[...] = jnp.dot(
        operator, by_slot(place_ref), preferred_element_type=jnp.float32
    ).astype(operator.dtype)


def first_kernel(place_ref, placed_ref, own_image_ref, *refs):
    half = len(refs) // 2
    got_refs, (image_ref, *send_refs) = refs[:half], refs[half:]
    height = got_refs[1].shape[0]
    got = spread(received(*got_refs), height - GROUP, (image_ref.shape[0] - height) // GROUP + 1)
    image = own_image_ref[...] - split_dot(got, placed_ref[...], NT)
    image_ref[...] = image
    send_blocks(image, place_ref, *send_refs)


def products_of(left, right):
    both = lax.dot_general(split(left), split(right), NT, preferred_element_type=jnp.float32)
    both = both[: left.shape[0]] + both[left.shape[0] :]
    return both + pltpu.roll(both, right.shape[0], 1)


def with_scalars(top, products, lanes):
    lane = lax.broadcasted_iota(jnp.int32, top.shape, 1)
    for at, product in zip(lanes, products):
        top = jnp.where(lane == at, jnp.sum(product, axis=1, keepdims=True), top)
    return top


def middle_kernel(place_ref, operator_ref, own_ref, image_ref, *refs):
    *got_refs, basis_ref, twice_ref, terms_ref = refs
    coarse = terms_ref.shape[1] // 8
    loads = own_ref.shape[0] - coarse
    got = spread(received(*got_refs), loads, coarse // GROUP)
    basis = own_ref[...] - split_dot(got, by_slot(place_ref), NT)
    basis_ref[...] = basis
    image = image_ref[...]
    twice_ref[...] = split_dot(image, operator_ref[0], NT)
    left = jnp.concatenate([basis[:loads], image[:loads], basis[loads:]])
    empty = jnp.zeros((2 * coarse, basis.shape[1]), jnp.float32)
    both = products_of(left, jnp.concatenate([basis[loads:], image[loads:], empty]))
    strip = lax.broadcasted_iota(jnp.int32, (loads, 8 * coarse), 1) // coarse
    top = jnp.where(strip < 2, both[:loads], 0.0)
    top = jnp.where(strip == 4, both[loads : 2 * loads], top)
    residual = basis[:loads]
    terms_ref[:loads] = with_scalars(top, (residual * residual, residual * image[:loads]), SCALAR_LANES[:2])
    strip = lax.broadcasted_iota(jnp.int32, (coarse, 8 * coarse), 1) // coarse
    terms_ref[loads:] = jnp.where(strip < 2, both[2 * loads :], 0.0)


def second_kernel(place_ref, placed_ref, basis_ref, image_ref, twice_ref, early_ref, *refs):
    *got_refs, jump_ref, terms_ref = refs
    coarse = terms_ref.shape[1] // 8
    loads = basis_ref.shape[0] - coarse
    got = received(*got_refs)
    jump = image_ref[...] - split_dot(got, by_slot(place_ref), NT)
    second = twice_ref[...] - split_dot(got, placed_ref[...], NT)
    jump_ref[...] = jump
    basis = basis_ref[...]
    left = jnp.concatenate([basis[:loads], jump[:loads], second[:loads], basis[loads:], jump[loads:]])
    empty = jnp.zeros((coarse, basis.shape[1]), jnp.float32)
    both = products_of(left, jnp.concatenate([basis[loads:], empty, jump[loads:], second[loads:]]))
    along, jumped, doubled = (both[at * loads : (at + 1) * loads] for at in range(3))
    base, far = both[3 * loads : 3 * loads + coarse], both[3 * loads + coarse :]
    strip = lax.broadcasted_iota(jnp.int32, (loads, 8 * coarse), 1) // coarse
    top = jnp.where(strip == 2, doubled, 0.0)
    top = jnp.where(strip == 3, along, top)
    top = jnp.where(strip == 5, pltpu.roll(doubled, coarse, 1), top)
    top = jnp.where(strip >= 6, jumped, top)
    residual, jump_loads, second_loads = basis[:loads], jump[:loads], second[:loads]
    products = (jump_loads * jump_loads, jump_loads * second_loads, residual * second_loads)
    terms_ref[:loads] = early_ref[:loads] + with_scalars(top, products, SCALAR_LANES[2:])
    strip = lax.broadcasted_iota(jnp.int32, (coarse, 8 * coarse), 1) // coarse
    base = jnp.where((strip == 2) | (strip == 3), base, 0.0)
    terms_ref[loads:] = early_ref[loads:] + jnp.where(strip < 4, base, far)


def eliminate(work, coarse):
    row = lax.broadcasted_iota(jnp.int32, work.shape, 0)
    for first in range(coarse):
        if first % 2 or first % GROUP >= MODES:
            continue
        second = first + 1
        left = jnp.broadcast_to(work[:, first : first + 1], work.shape)
        right = jnp.broadcast_to(work[:, second : second + 1], work.shape)
        upper, lower = work[first : first + 1], work[second : second + 1]
        pivot = 1.0 / left[first : first + 1]
        ratio = left[second : second + 1] * pivot
        corner = 1.0 / (right[second : second + 1] - ratio * right[first : first + 1])
        lower = (lower - ratio * upper) * corner
        upper = (upper - right[first : first + 1] * lower) * pivot
        work = work - left * upper - right * lower
        work = jnp.where(row == first, upper, jnp.where(row == second, lower, work))
    return work


def thin_dot(left, right):
    high, right_high = (value.astype(jnp.bfloat16).astype(jnp.float32) for value in (left, right))
    return jnp.dot(
        jnp.concatenate([high, left - high, high], axis=1).astype(jnp.bfloat16),
        jnp.concatenate([right_high, right_high, right - right_high], axis=0).astype(jnp.bfloat16),
        preferred_element_type=jnp.float32,
    )


def final_kernel(terms_ref, basis_ref, jump_ref, multipliers_ref, amplitudes_ref):
    coarse = terms_ref.shape[1] // 8
    loads = basis_ref.shape[0] - coarse
    groups = coarse // GROUP
    by_load = terms_ref[:loads].T
    used = lax.broadcasted_iota(jnp.int32, (coarse, loads), 0) % GROUP < MODES

    def strip(at):
        return by_load[at * coarse : (at + 1) * coarse]

    def block(at):
        return terms_ref[loads:, at * coarse : (at + 1) * coarse]

    def total(values):
        return jnp.sum(values, axis=0, keepdims=True)

    res_res, res_image, jump_jump, jump_second, res_second = (by_load[at : at + 1] for at in SCALAR_LANES)
    coarse_res, res_h = (jnp.where(used, strip(at), 0.0) for at in (0, 1))
    second_z, res_dz, image_g, second_g, jump_z, jump_dz = (strip(at) for at in range(2, 8))
    g_h, g_dz, z_z, z_dz = block(1), block(3), block(6), block(7)
    row = lax.broadcasted_iota(jnp.int32, (coarse, coarse), 0)
    unit = jnp.where(row == lax.broadcasted_iota(jnp.int32, (coarse, coarse), 1), 1.0, 0.0)
    empty = jnp.zeros((coarse, 5 * coarse - 2 * loads), jnp.float32)
    solved = eliminate(
        jnp.concatenate([terms_ref[loads:, : 2 * coarse], coarse_res, image_g, unit, empty], axis=1), coarse
    )
    inverse_h = solved[:, coarse : 2 * coarse]
    amounts = solved[:, 2 * coarse : 2 * coarse + loads]
    inverse_image = solved[:, 2 * coarse + loads : 2 * coarse + 2 * loads]
    inverse = solved[:, 2 * coarse + 2 * loads : 3 * coarse + 2 * loads]
    products = small_dot(jnp.concatenate([inverse_h, g_h, z_z, g_dz, z_dz], axis=0), amounts)
    inverse_h_amounts, h_amounts, z_amounts, g_dz_amounts, z_dz_amounts = (
        products[at * coarse : (at + 1) * coarse] for at in range(5)
    )
    shares = 2.0 * (inverse_image - inverse_h_amounts)
    both = jnp.concatenate([amounts, shares], axis=0).T
    basis_g, jump_z_rows = basis_ref[loads:], jump_ref[loads:]
    d = basis_ref[:loads] - thin_dot(both[:, :coarse], basis_g)
    u = jump_ref[:loads] - thin_dot(both, jnp.concatenate([jump_z_rows, basis_g], axis=0))
    products = small_dot(jnp.concatenate([g_h, z_z], axis=0), shares)
    image_d = image_g - h_amounts
    inner = res_res - total(amounts * coarse_res)
    curvature = 2.0 * (res_image - total(amounts * (res_h + image_d)))
    u_u = jump_jump - total(amounts * (2.0 * jump_z - z_amounts) + 2.0 * image_d * shares)
    second_u = second_g - g_dz_amounts - products[:coarse]
    jump_u = second_z - z_dz_amounts - 0.5 * products[coarse:]
    d_second = res_second - total(amounts * (res_dz + second_u) + shares * res_h)
    u_second = jump_second - total(amounts * (jump_dz + jump_u) + shares * (0.5 * jump_z + second_u))
    step = inner / curvature
    renewed = step * step * u_u - inner
    grown = 1.0 + renewed / inner
    curvature = grown * grown * curvature - grown * step * (2.0 * d_second + u_u) + 2.0 * step * step * u_second
    second_step = renewed / curvature
    on_d, on_u = step + second_step * grown, second_step * step
    amplitudes = amounts - on_d * shares + 2.0 * on_u * small_dot(inverse, second_u)
    amplitudes_ref[...] = jnp.concatenate(
        [amplitudes[label * GROUP : label * GROUP + MODES] for label in range(groups)], axis=0
    )
    weights = jnp.concatenate([on_d, on_u, jnp.zeros((6, loads), jnp.float32)], axis=0).T
    multipliers_ref[...] = weights[:, 0:1] * d - weights[:, 1:2] * u


def call(kernel, shapes, in_specs, name, scratch=(), flops=0):
    return pl.pallas_call(
        kernel,
        out_shape=[jax.ShapeDtypeStruct(*shape) for shape in shapes],
        in_specs=in_specs,
        out_specs=[VMEM] * len(shapes),
        scratch_shapes=scratch,
        compiler_params=pltpu.CompilerParams(vmem_limit_bytes=24 * 1024 * 1024),
        cost_estimate=pl.CostEstimate(flops=flops, bytes_accessed=2**20, transcendentals=0),
        name=name,
    )


def permute(values, offset, plane_offset=0):
    peers, planes = lax.axis_size("sub"), lax.axis_size("rep")
    offset = offset * planes + plane_offset
    return lax.ppermute(values, ("sub", "rep"), [(at, at ^ offset) for at in range(peers * planes)])


def exchange(near, own, *pairs):
    height = own.shape[0]
    pairs = [permute(pair, 2 * (len(pairs) - at) + 1) for at, pair in enumerate(pairs)]
    near = permute(jnp.concatenate([near, *(pair[height:] for pair in pairs)], axis=0), 1)
    return near, own, *pairs


def total(terms):
    chips = [(offset + 1, 0) for offset in range(2, lax.axis_size("sub"), 2)]
    planes = [(1, offset) for offset in range(1, lax.axis_size("rep"))]
    for offsets in ([(1, 0)], chips, planes):
        parts = [terms, *(permute(terms, *offset) for offset in offsets)]
        while len(parts) > 1:
            parts = [low + high for low, high in zip(parts[::2], parts[1::2])]
        terms = parts[0]
    return terms


def fused_body(dual_ops, mode_traces, route, mode_block, local_gap):
    peers = lax.axis_size("sub")
    loads, rows = local_gap.shape
    modes = mode_traces.shape[1]
    subs = mode_block.shape[0]
    groups = subs // AGG_SUBS
    per_peer = rows // peers
    height = loads + GROUP * groups
    f32, i32 = jnp.float32, jnp.int32
    tall = ((height, rows), f32)
    wide = ((height, 8 * GROUP * groups), f32)

    def blocks(height):
        return [((height, per_peer), f32)] * 2 + [((2 * height, per_peer), f32)] * (peers // 2 - 1)

    def held(value):
        return pltpu.with_memory_space_constraint(value, pltpu.HBM)

    matrix = ((rows, rows), dual_ops.dtype)
    inputs = [route, mode_block.reshape(1, subs), local_gap, mode_traces.transpose(1, 0, 2)]
    place, values, *send = call(
        place_kernel,
        [((rows, rows + per_peer), jnp.bfloat16), ((loads + GROUP, rows), f32), *blocks(loads + GROUP)],
        [HBM] * 4,
        "place",
        [
            pltpu.VMEM((1, rows), i32),
            pltpu.VMEM((1, subs), i32),
            pltpu.VMEM((modes, 1, rows), f32),
            pltpu.SemaphoreType.DMA((4,)),
        ],
    )(*(held(value) for value in inputs))
    got = exchange(*send)
    operator, placed, own, own_image = call(
        ready_kernel,
        [(dual_ops.shape, dual_ops.dtype), matrix, tall, tall],
        [HBM, VMEM, VMEM],
        "ready",
        [pltpu.SemaphoreType.DMA],
        2 * rows * rows * (rows + 2 * height),
    )(held(dual_ops), place, values)
    image, *send = call(first_kernel, [tall, *blocks(height)], [VMEM] * (3 + len(got)), "first")(
        place, placed, own_image, *got
    )
    got_image = exchange(*send)
    basis, twice, terms = call(
        middle_kernel,
        [tall, tall, wide],
        [VMEM] * (4 + len(got)),
        "middle",
        flops=8 * rows * rows * height,
    )(place, operator, own, image, *got)
    jump, terms = call(second_kernel, [tall, wide], [VMEM] * (6 + len(got)), "second")(
        place, placed, basis, image, twice, terms, *got_image
    )
    multipliers, amplitudes = call(
        final_kernel, [((loads, rows), f32), ((MODES * groups, loads), f32)], [VMEM] * 3, "final"
    )(total(terms), basis, jump)
    return multipliers, amplitudes.T


def general_body(dual_ops, mode_traces, route, mode_block, local_gap):
    own_index = lax.axis_index("sub")
    plane_index = lax.axis_index("rep")
    peer_count = lax.axis_size("sub")
    plane_count = lax.axis_size("rep")
    operator = dual_ops[0]
    traces = mode_traces[0]
    slot_rows = route[0]
    rows_here = operator.shape[0]
    load_cases = local_gap.shape[0]
    per_peer = rows_here // peer_count
    blocks = mode_block[:, 0]
    block_count = blocks.shape[0] // AGG_SUBS
    coarse = block_count * MODES
    positions = jnp.arange(rows_here, dtype=jnp.int32)
    inverse = jnp.zeros((rows_here,), jnp.int32).at[slot_rows].set(positions)
    slot_peer = positions // per_peer
    within = positions % per_peer
    flip_index = jnp.where(
        slot_peer == own_index, slot_peer * per_peer + per_peer - 1 - within, positions
    )
    peer_ids = jnp.arange(peer_count, dtype=jnp.int32)
    peer_blocks = blocks[peer_ids * plane_count + plane_index]
    own_block = blocks[own_index * plane_count + plane_index]
    labels = jnp.arange(block_count, dtype=jnp.int32)
    peer_onehot = (peer_blocks[:, None] == labels[None, :]).astype(jnp.float32)
    own_onehot = (labels == own_block).astype(jnp.float32)
    trace_slots = traces[:, slot_rows]
    receive_index = flip_index[inverse]

    def to_peers(values):
        return values[:, slot_rows]

    def from_peers(values):
        return values[:, inverse]

    gap_peers = to_peers(local_gap)
    got_traces = lax.all_to_all(trace_slots, "sub", split_axis=1, concat_axis=1, tiled=True)
    got_gap = lax.all_to_all(gap_peers, "sub", split_axis=1, concat_axis=1, tiled=True)
    partner_traces = got_traces[:, flip_index]
    residual = local_gap - got_gap[:, receive_index]
    own_gram = jnp.dot(traces, traces.T, precision=HIGHEST)
    paired = (trace_slots[:, None, :] * partner_traces[None, :, :]).reshape(
        MODES, MODES, peer_count, per_peer
    )
    cross_terms = jnp.sum(paired, axis=3)
    cross_blocks = jnp.einsum("klq,qb->kbl", cross_terms, peer_onehot, precision=HIGHEST)
    own_blocks = own_gram[:, None, :] * own_onehot[None, :, None]
    row_term = 2.0 * (own_blocks - cross_blocks).reshape(MODES, coarse)
    gram_term = (own_onehot[:, None, None] * row_term[None]).reshape(coarse, coarse)

    def coarse_term(values):
        own_part = 2.0 * jnp.dot(values, traces.T, precision=HIGHEST)
        return (own_part[:, None, :] * own_onehot[None, :, None]).reshape(load_cases, coarse)

    def expand(amounts):
        grouped = amounts.reshape(load_cases, block_count, MODES)
        own_amounts = lax.dynamic_index_in_dim(grouped, own_block, 1, keepdims=False)
        own_part = jnp.dot(own_amounts, traces, precision=HIGHEST)
        peer_amounts = jnp.einsum("qb,rbk->rkq", peer_onehot, grouped, precision=HIGHEST)
        spread = jnp.repeat(peer_amounts, per_peer, axis=2)
        peer_part = jnp.sum(spread * partner_traces[None, :, :], axis=1)
        return own_part - from_peers(peer_part)

    squares = jnp.sum(residual * residual, axis=1)
    gram_matrix, coarse_res, norm_res = lax.psum(
        (gram_term, coarse_term(residual), squares), ("sub", "rep")
    )
    factor = jnp.linalg.cholesky(gram_matrix)

    def solve_coarse(right):
        return jax.scipy.linalg.cho_solve((factor, True), right.T).T

    amplitudes = solve_coarse(coarse_res)
    projected = residual - expand(amplitudes)
    inner_sum = norm_res - jnp.sum(amplitudes * coarse_res, axis=1)
    direction = projected
    multipliers = jnp.zeros_like(residual)
    for iteration in range(ITERS):
        product = lax.dot_general(
            direction.astype(jnp.bfloat16),
            operator,
            (((1,), (1,)), ((), ())),
            preferred_element_type=jnp.float32,
        )
        got_product = lax.all_to_all(
            to_peers(product), "sub", split_axis=1, concat_axis=1, tiled=True
        )
        image_jump = product - got_product[:, receive_index]
        coarse_jump, jump_squares, residual_cross, curvature = lax.psum(
            (
                coarse_term(image_jump),
                jnp.sum(image_jump * image_jump, axis=1),
                jnp.sum(residual * image_jump, axis=1),
                jnp.sum(direction * image_jump, axis=1),
            ),
            ("sub", "rep"),
        )
        step_size = inner_sum / curvature
        multipliers = multipliers + step_size[:, None] * direction
        residual = residual - step_size[:, None] * image_jump
        coarse_res = coarse_res - step_size[:, None] * coarse_jump
        norm_res = (
            norm_res - 2.0 * step_size * residual_cross + step_size * step_size * jump_squares
        )
        amplitudes = solve_coarse(coarse_res)
        if iteration + 1 < ITERS:
            projected = residual - expand(amplitudes)
            renewed = norm_res - jnp.sum(amplitudes * coarse_res, axis=1)
            direction = projected + (renewed / inner_sum)[:, None] * direction
            inner_sum = renewed
    return (multipliers, amplitudes)


def fits(mesh, dual_ops, mode_block, local_gap):
    peers, planes = mesh.shape["sub"], mesh.shape["rep"]
    powers = all(size & (size - 1) == 0 for size in (peers, planes))
    whole = dual_ops.shape[1] % (128 * peers) == 0 and local_gap.shape[0] % 16 == 0
    return powers and whole and 8 * GROUP * (mode_block.shape[0] // AGG_SUBS) == 128


def solution(mesh):
    placed = (
        P(("sub", "rep"), None, None),
        P(("sub", "rep"), None, None),
        P(("sub", "rep"), None),
        P(),
        P(None, ("sub", "rep")),
    )

    def run(dual_ops, mode_traces, route, mode_block, local_gap):
        body = fused_body if fits(mesh, dual_ops, mode_block, local_gap) else general_body
        return jax.shard_map(
            body, mesh=mesh, in_specs=placed, out_specs=(P(None, ("sub", "rep")), P()), check_vma=False
        )(dual_ops, mode_traces, route, mode_block, local_gap)

    return run
```

profile of v0, /device:TPU:0, one launch (start us, length us, event | category | flops | bytes accessed | tf_op | source)
XLA Modules:
  0.0 43.6 jit_solution(9590319249727171726)
XLA Ops:
  0.6 2.3 %place.1 = (bf16[1024,1152]{1,0:T(8,128)(2,1)S(1)}, f32[40,1024]{1,0:T(8,128)S(1)}, f32[40,128]{1,0:T(8,128)S(1)}, f32[40,128]{1,0:T(8,128)S(1)}, f32[80,128]{1,...) custom-call(s32[1,1024]{1,0:T(1,128)} %route_hbm.1, s32[1,32]{1,0:T(1,128)} %bitcast.4, f32[32,1024]{1,0:T(8,128)} %gap_hbm.1, ...), custom_call_target="tpu_custom_call" | custom-call | bytes 1048576 | tf_op jit(solution)/shard_map/place/pallas_call | solution.py:353
  3.0 3.4 %collective-permute-start = (f32[80,128]{1,0:T(8,128)S(1)}, f32[80,128]{1,0:T(8,128)S(1)}, u32[]{:S(2)}, u32[]{:S(2)}) collective-permute-start(f32[80,128]{1,0:T(8,128)S(1)} %get-tuple-element.33), channel_id=1, source_target_pairs={{0,28},{1,29},{2,30},{3,31},{4,24},{5,25},{6,26},{7,27},{8,20},{9,... | collective-permute-start | bytes 122888 | tf_op jit(solution)/shard_map/ppermute | solution.py:312
  6.4 0.8 %collective-permute-start.1 = (f32[80,128]{1,0:T(8,128)S(1)}, f32[80,128]{1,0:T(8,128)S(1)}, u32[]{:S(2)}, u32[]{:S(2)}) collective-permute-start(f32[80,128]{1,0:T(8,128)S(1)} %get-tuple-element.34), channel_id=1, source_target_pairs={{0,20},{1,21},{2,22},{3,23},{4,16},{5,17},{6,18},{7,19},{8,28},{9,... | collective-permute-start | bytes 122888 | tf_op jit(solution)/shard_map/ppermute | solution.py:312
  7.2 0.1 collective-permute-start.2
  7.3 1.0 %collective-permute-done.refs_2_ = f32[80,128]{1,0:T(8,128)S(1)} collective-permute-done((f32[80,128]{1,0:T(8,128)S(1)}, f32[80,128]{1,0:T(8,128)S(1)}, u32[]{:S(2)}, u32[]{:S(2)}) %collective-permute-start) | collective-permute-done | bytes 40992 | tf_op jit(solution)/shard_map/ppermute | solution.py:312
  8.3 1.5 %collective-permute-done.1.refs_3_ = f32[80,128]{1,0:T(8,128)S(1)} collective-permute-done((f32[80,128]{1,0:T(8,128)S(1)}, f32[80,128]{1,0:T(8,128)S(1)}, u32[]{:S(2)}, u32[]{:S(2)}) %collective-permute-start.1) | collective-permute-done | bytes 40992 | tf_op jit(solution)/shard_map/ppermute | solution.py:312
  9.8 1.2 %collective-permute-done.2.refs_4_ = f32[80,128]{1,0:T(8,128)S(1)} collective-permute-done((f32[80,128]{1,0:T(8,128)S(1)}, f32[80,128]{1,0:T(8,128)S(1)}, u32[]{:S(2)}, u32[]{:S(2)}) %collective-permute-start.2) | collective-permute-done | bytes 40992 | tf_op jit(solution)/shard_map/ppermute | solution.py:312
  11.0 0.2 collective-permute-start.3
  11.2 4.6 %ready.1 = (bf16[1,1024,1024]{2,1,0:T(8,128)(2,1)S(1)}, bf16[1024,1024]{1,0:T(8,128)(2,1)S(1)}, f32[48,1024]{1,0:T(8,128)S(1)}, f32[48,1024]{1,0:T(8,128)S(1)}) custom-call(bf16[1,1024,1024]{2,1,0:T(8,128)(2,1)} %operator_hbm.1, bf16[1024,1152]{1,0:T(8,128)(2,1)S(1)} %get-tuple-element.26.place_ref, f32[40,1024]{1,0:T(8,128)S(1)} %get-tuple-element.27.values_ref), custom_call_target="tpu_custom_call" | custom-call | flops 2348810240 | bytes 1048576 | tf_op jit(solution)/shard_map/ready/pallas_call | solution.py:366
  15.7 0.0 collective-permute-done.3.refs_0_
  15.7 1.1 %first.1 = (f32[48,1024]{1,0:T(8,128)S(1)}, f32[48,128]{1,0:T(8,128)S(1)}, f32[48,128]{1,0:T(8,128)S(1)}, f32[96,128]{1,0:T(8,128)S(1)}, f32[96,128]{1,0:T(8,128)S(1)}, /*index=5*/f32[96,128]{1,0:T(8,128)S(1)}) custom-call(bf16[1024,1152]{1,0:T(8,128)(2,1)S(1)} %get-tuple-element.26.place_ref, bf16[1024,1024]{1,0:T(8,128)(2,1)S(1)} %get-tuple-element.28.placed_ref, ...), custom_call_target="tpu_custom_call" | custom-call | bytes 1048576 | tf_op jit(solution)/shard_map/first/pallas_call | solution.py:374
  16.9 1.6 %collective-permute-start.4 = (f32[96,128]{1,0:T(8,128)S(1)}, f32[96,128]{1,0:T(8,128)S(1)}, u32[]{:S(2)}, u32[]{:S(2)}) collective-permute-start(f32[96,128]{1,0:T(8,128)S(1)} %get-tuple-element.42), channel_id=1, source_target_pairs={{0,28},{1,29},{2,30},{3,31},{4,24},{5,25},{6,26},{7,27},{8,20},{9,... | collective-permute-start | bytes 147464 | tf_op jit(solution)/shard_map/ppermute | solution.py:312
  18.5 0.3 collective-permute-start.5
  18.8 1.3 %collective-permute-start.6 = (f32[96,128]{1,0:T(8,128)S(1)}, f32[96,128]{1,0:T(8,128)S(1)}, u32[]{:S(2)}, u32[]{:S(2)}) collective-permute-start(f32[96,128]{1,0:T(8,128)S(1)} %get-tuple-element.44), channel_id=1, source_target_pairs={{0,12},{1,13},{2,14},{3,15},{4,8},{5,9},{6,10},{7,11},{8,4},{9,5},... | collective-permute-start | bytes 147464 | tf_op jit(solution)/shard_map/ppermute | solution.py:312
  20.1 1.2 %collective-permute-done.4.refs_2_ = f32[96,128]{1,0:T(8,128)S(1)} collective-permute-done((f32[96,128]{1,0:T(8,128)S(1)}, f32[96,128]{1,0:T(8,128)S(1)}, u32[]{:S(2)}, u32[]{:S(2)}) %collective-permute-start.4) | collective-permute-done | bytes 49184 | tf_op jit(solution)/shard_map/ppermute | solution.py:312
  21.4 1.6 %collective-permute-done.5.refs_3_ = f32[96,128]{1,0:T(8,128)S(1)} collective-permute-done((f32[96,128]{1,0:T(8,128)S(1)}, f32[96,128]{1,0:T(8,128)S(1)}, u32[]{:S(2)}, u32[]{:S(2)}) %collective-permute-start.5) | collective-permute-done | bytes 49184 | tf_op jit(solution)/shard_map/ppermute | solution.py:312
  22.9 0.0 collective-permute-done.6.refs_4_
  23.0 0.2 collective-permute-start.7
  23.2 1.6 %middle.1 = (f32[48,1024]{1,0:T(8,128)S(1)}, f32[48,1024]{1,0:T(8,128)S(1)}, f32[48,128]{1,0:T(8,128)S(1)}) custom-call(bf16[1024,1152]{1,0:T(8,128)(2,1)S(1)} %get-tuple-element.26.place_ref, bf16[1,1024,1024]{2,1,0:T(8,128)(2,1)S(1)} %get-tuple-element.29.operator_ref, f32[48,1024]{1,0:T(8,128)S(1)} %get-tuple-element.30.own_ref, ...), custom_call_target="tpu_custom_call" | custom-call | flops 402653184 | bytes 1048576 | tf_op jit(solution)/shard_map/middle/pallas_call | solution.py:378
  24.7 0.0 collective-permute-done.7.refs_0_
  24.7 1.9 %second.1 = (f32[48,1024]{1,0:T(8,128)S(1)}, f32[48,128]{1,0:T(8,128)S(1)}) custom-call(bf16[1024,1152]{1,0:T(8,128)(2,1)S(1)} %get-tuple-element.26.place_ref, bf16[1024,1024]{1,0:T(8,128)(2,1)S(1)} %get-tuple-element.28.placed_ref, f32[48,1024]{1,0:T(8,128)S(1)} %get-tuple-element.38.basis_ref, f32[48,1024]{1,0:T(8,128)S(1)} %get-tuple-element.37.image_ref, ...), custom_call_target="tpu_custom_call" | custom-call | bytes 1048576 | tf_op jit(solution)/shard_map/second/pallas_call | solution.py:385
  26.6 0.5 %collective-permute-start.8 = (f32[48,128]{1,0:T(8,128)S(1)}, f32[48,128]{1,0:T(8,128)S(1)}, u32[]{:S(2)}, u32[]{:S(2)}) collective-permute-start(f32[48,128]{1,0:T(8,128)S(1)} %get-tuple-element.46), channel_id=1, source_target_pairs={{0,4},{1,5},{2,6},{3,7},{4,0},{5,1},{6,2},{7,3},{8,12},{9,13},{10,... | collective-permute-start | bytes 73736 | tf_op jit(solution)/shard_map/ppermute | solution.py:312
  27.1 0.8 %collective-permute-done.8 = f32[48,128]{1,0:T(8,128)S(1)} collective-permute-done((f32[48,128]{1,0:T(8,128)S(1)}, f32[48,128]{1,0:T(8,128)S(1)}, u32[]{:S(2)}, u32[]{:S(2)}) %collective-permute-start.8) | collective-permute-done | bytes 24608 | tf_op jit(solution)/shard_map/ppermute | solution.py:312
  27.9 1.7 %collective-permute-start.11 = (f32[48,128]{1,0:T(8,128)S(1)}, f32[48,128]{1,0:T(8,128)S(1)}, u32[]{:S(2)}, u32[]{:S(2)}) collective-permute-start(f32[48,128]{1,0:T(8,128)S(1)} %add.21), channel_id=1, source_target_pairs={{0,28},{1,29},{2,30},{3,31},{4,24},{5,25},{6,26},{7,27},{8,20},{9,... | collective-permute-start | bytes 73736 | tf_op jit(solution)/shard_map/ppermute | solution.py:312
  29.7 0.4 collective-permute-start.10
  30.0 1.1 %collective-permute-start.9 = (f32[48,128]{1,0:T(8,128)S(1)}, f32[48,128]{1,0:T(8,128)S(1)}, u32[]{:S(2)}, u32[]{:S(2)}) collective-permute-start(f32[48,128]{1,0:T(8,128)S(1)} %add.21), channel_id=1, source_target_pairs={{0,12},{1,13},{2,14},{3,15},{4,8},{5,9},{6,10},{7,11},{8,4},{9,5},... | collective-permute-start | bytes 73736 | tf_op jit(solution)/shard_map/ppermute | solution.py:312
  31.1 1.0 %collective-permute-done.11 = f32[48,128]{1,0:T(8,128)S(1)} collective-permute-done((f32[48,128]{1,0:T(8,128)S(1)}, f32[48,128]{1,0:T(8,128)S(1)}, u32[]{:S(2)}, u32[]{:S(2)}) %collective-permute-start.11) | collective-permute-done | bytes 24608 | tf_op jit(solution)/shard_map/ppermute | solution.py:312
  32.1 0.8 %collective-permute-done.10 = f32[48,128]{1,0:T(8,128)S(1)} collective-permute-done((f32[48,128]{1,0:T(8,128)S(1)}, f32[48,128]{1,0:T(8,128)S(1)}, u32[]{:S(2)}, u32[]{:S(2)}) %collective-permute-start.10) | collective-permute-done | bytes 24608 | tf_op jit(solution)/shard_map/ppermute | solution.py:312
  32.9 0.4 collective-permute-done.9
  33.3 3.5 %collective-permute-start.14 = (f32[48,128]{1,0:T(8,128)S(1)}, f32[48,128]{1,0:T(8,128)S(1)}, u32[]{:S(2)}, u32[]{:S(2)}) collective-permute-start(f32[48,128]{1,0:T(8,128)S(1)} %add_add_fusion.1), channel_id=1, source_target_pairs={{0,7},{1,6},{2,5},{3,4},{4,3},{5,2},{6,1},{7,0},{8,15},{9,14},{10,... | collective-permute-start | bytes 73736 | tf_op jit(solution)/shard_map/ppermute | solution.py:312
  36.8 0.0 collective-permute-start.13
  36.8 0.5 %collective-permute-start.12 = (f32[48,128]{1,0:T(8,128)S(1)}, f32[48,128]{1,0:T(8,128)S(1)}, u32[]{:S(2)}, u32[]{:S(2)}) collective-permute-start(f32[48,128]{1,0:T(8,128)S(1)} %add_add_fusion.1), channel_id=1, source_target_pairs={{0,5},{1,4},{2,7},{3,6},{4,1},{5,0},{6,3},{7,2},{8,13},{9,12},{10,... | collective-permute-start | bytes 73736 | tf_op jit(solution)/shard_map/ppermute | solution.py:312
  37.3 1.1 %collective-permute-done.14 = f32[48,128]{1,0:T(8,128)S(1)} collective-permute-done((f32[48,128]{1,0:T(8,128)S(1)}, f32[48,128]{1,0:T(8,128)S(1)}, u32[]{:S(2)}, u32[]{:S(2)}) %collective-permute-start.14) | collective-permute-done | bytes 24608 | tf_op jit(solution)/shard_map/ppermute | solution.py:312
  38.4 2.6 %collective-permute-done.13 = f32[48,128]{1,0:T(8,128)S(1)} collective-permute-done((f32[48,128]{1,0:T(8,128)S(1)}, f32[48,128]{1,0:T(8,128)S(1)}, u32[]{:S(2)}, u32[]{:S(2)}) %collective-permute-start.13) | collective-permute-done | bytes 24608 | tf_op jit(solution)/shard_map/ppermute | solution.py:312
  41.0 0.0 collective-permute-done.12
  41.0 2.6 %final.1 = (f32[32,1024]{1,0:T(8,128)}, f32[12,32]{1,0:T(8,128)}) custom-call(f32[48,128]{1,0:T(8,128)S(1)} %add_add_fusion.terms_ref, f32[48,1024]{1,0:T(8,128)S(1)} %get-tuple-element.38.basis_ref, f32[48,1024]{1,0:T(8,128)S(1)} %get-tuple-element.47.jump_ref), custom_call_target="tpu_custom_call" | custom-call | bytes 1048576 | tf_op jit(solution)/shard_map/final/pallas_call | solution.py:388
  (11 shorter events, 0.1 us)
Async XLA Ops:
  3.0 5.4 %collective-permute-start = (f32[80,128]{1,0:T(8,128)S(1)}, f32[80,128]{1,0:T(8,128)S(1)}, u32[]{:S(2)}, u32[]{:S(2)}) collective-permute-start(f32[80,128]{1,0:T(8,128)S(1)} %get-tuple-element.33), channel_id=1, source_target_pairs={{0,28},{1,29},{2,30},{3,31},{4,24},{5,25},{6,26},{7,27},{8,20},{9,... | collective-permute-start | bytes 122888 | tf_op jit(solution)/shard_map/ppermute | solution.py:312
  6.4 3.4 %collective-permute-start.1 = (f32[80,128]{1,0:T(8,128)S(1)}, f32[80,128]{1,0:T(8,128)S(1)}, u32[]{:S(2)}, u32[]{:S(2)}) collective-permute-start(f32[80,128]{1,0:T(8,128)S(1)} %get-tuple-element.34), channel_id=1, source_target_pairs={{0,20},{1,21},{2,22},{3,23},{4,16},{5,17},{6,18},{7,19},{8,28},{9,... | collective-permute-start | bytes 122888 | tf_op jit(solution)/shard_map/ppermute | solution.py:312
  7.2 3.8 %collective-permute-start.2 = (f32[80,128]{1,0:T(8,128)S(1)}, f32[80,128]{1,0:T(8,128)S(1)}, u32[]{:S(2)}, u32[]{:S(2)}) collective-permute-start(f32[80,128]{1,0:T(8,128)S(1)} %get-tuple-element.35), channel_id=1, source_target_pairs={{0,12},{1,13},{2,14},{3,15},{4,8},{5,9},{6,10},{7,11},{8,4},{9,5},... | collective-permute-start | bytes 122888 | tf_op jit(solution)/shard_map/ppermute | solution.py:312
  11.0 4.8 %collective-permute-start.3 = (f32[160,128]{1,0:T(8,128)S(1)}, f32[160,128]{1,0:T(8,128)S(1)}, u32[]{:S(2)}, u32[]{:S(2)}) collective-permute-start(f32[160,128]{1,0:T(8,128)S(1)} %pad_maximum_fusion.1), channel_id=1, source_target_pairs={{0,4},{1,5},{2,6},{3,7},{4,0},{5,1},{6,2},{7,3},{8,12},{9,13},{10,... | collective-permute-start | bytes 245768 | tf_op jit(solution)/shard_map/ppermute | solution.py:312
  16.9 4.5 %collective-permute-start.4 = (f32[96,128]{1,0:T(8,128)S(1)}, f32[96,128]{1,0:T(8,128)S(1)}, u32[]{:S(2)}, u32[]{:S(2)}) collective-permute-start(f32[96,128]{1,0:T(8,128)S(1)} %get-tuple-element.42), channel_id=1, source_target_pairs={{0,28},{1,29},{2,30},{3,31},{4,24},{5,25},{6,26},{7,27},{8,20},{9,... | collective-permute-start | bytes 147464 | tf_op jit(solution)/shard_map/ppermute | solution.py:312
  18.5 4.5 %collective-permute-start.5 = (f32[96,128]{1,0:T(8,128)S(1)}, f32[96,128]{1,0:T(8,128)S(1)}, u32[]{:S(2)}, u32[]{:S(2)}) collective-permute-start(f32[96,128]{1,0:T(8,128)S(1)} %get-tuple-element.43), channel_id=1, source_target_pairs={{0,20},{1,21},{2,22},{3,23},{4,16},{5,17},{6,18},{7,19},{8,28},{9,... | collective-permute-start | bytes 147464 | tf_op jit(solution)/shard_map/ppermute | solution.py:312
  18.8 4.1 %collective-permute-start.6 = (f32[96,128]{1,0:T(8,128)S(1)}, f32[96,128]{1,0:T(8,128)S(1)}, u32[]{:S(2)}, u32[]{:S(2)}) collective-permute-start(f32[96,128]{1,0:T(8,128)S(1)} %get-tuple-element.44), channel_id=1, source_target_pairs={{0,12},{1,13},{2,14},{3,15},{4,8},{5,9},{6,10},{7,11},{8,4},{9,5},... | collective-permute-start | bytes 147464 | tf_op jit(solution)/shard_map/ppermute | solution.py:312
  23.0 1.8 %collective-permute-start.7 = (f32[192,128]{1,0:T(8,128)S(1)}, f32[192,128]{1,0:T(8,128)S(1)}, u32[]{:S(2)}, u32[]{:S(2)}) collective-permute-start(f32[192,128]{1,0:T(8,128)S(1)} %pad_maximum_fusion), channel_id=1, source_target_pairs={{0,4},{1,5},{2,6},{3,7},{4,0},{5,1},{6,2},{7,3},{8,12},{9,13},{10,... | collective-permute-start | bytes 294920 | tf_op jit(solution)/shard_map/ppermute | solution.py:312
  26.6 1.3 %collective-permute-start.8 = (f32[48,128]{1,0:T(8,128)S(1)}, f32[48,128]{1,0:T(8,128)S(1)}, u32[]{:S(2)}, u32[]{:S(2)}) collective-permute-start(f32[48,128]{1,0:T(8,128)S(1)} %get-tuple-element.46), channel_id=1, source_target_pairs={{0,4},{1,5},{2,6},{3,7},{4,0},{5,1},{6,2},{7,3},{8,12},{9,13},{10,... | collective-permute-start | bytes 73736 | tf_op jit(solution)/shard_map/ppermute | solution.py:312
  27.9 4.2 %collective-permute-start.11 = (f32[48,128]{1,0:T(8,128)S(1)}, f32[48,128]{1,0:T(8,128)S(1)}, u32[]{:S(2)}, u32[]{:S(2)}) collective-permute-start(f32[48,128]{1,0:T(8,128)S(1)} %add.21), channel_id=1, source_target_pairs={{0,28},{1,29},{2,30},{3,31},{4,24},{5,25},{6,26},{7,27},{8,20},{9,... | collective-permute-start | bytes 73736 | tf_op jit(solution)/shard_map/ppermute | solution.py:312
  29.7 3.3 %collective-permute-start.10 = (f32[48,128]{1,0:T(8,128)S(1)}, f32[48,128]{1,0:T(8,128)S(1)}, u32[]{:S(2)}, u32[]{:S(2)}) collective-permute-start(f32[48,128]{1,0:T(8,128)S(1)} %add.21), channel_id=1, source_target_pairs={{0,20},{1,21},{2,22},{3,23},{4,16},{5,17},{6,18},{7,19},{8,28},{9,... | collective-permute-start | bytes 73736 | tf_op jit(solution)/shard_map/ppermute | solution.py:312
  30.0 3.3 %collective-permute-start.9 = (f32[48,128]{1,0:T(8,128)S(1)}, f32[48,128]{1,0:T(8,128)S(1)}, u32[]{:S(2)}, u32[]{:S(2)}) collective-permute-start(f32[48,128]{1,0:T(8,128)S(1)} %add.21), channel_id=1, source_target_pairs={{0,12},{1,13},{2,14},{3,15},{4,8},{5,9},{6,10},{7,11},{8,4},{9,5},... | collective-permute-start | bytes 73736 | tf_op jit(solution)/shard_map/ppermute | solution.py:312
  33.3 5.1 %collective-permute-start.14 = (f32[48,128]{1,0:T(8,128)S(1)}, f32[48,128]{1,0:T(8,128)S(1)}, u32[]{:S(2)}, u32[]{:S(2)}) collective-permute-start(f32[48,128]{1,0:T(8,128)S(1)} %add_add_fusion.1), channel_id=1, source_target_pairs={{0,7},{1,6},{2,5},{3,4},{4,3},{5,2},{6,1},{7,0},{8,15},{9,14},{10,... | collective-permute-start | bytes 73736 | tf_op jit(solution)/shard_map/ppermute | solution.py:312
  36.8 4.2 %collective-permute-start.13 = (f32[48,128]{1,0:T(8,128)S(1)}, f32[48,128]{1,0:T(8,128)S(1)}, u32[]{:S(2)}, u32[]{:S(2)}) collective-permute-start(f32[48,128]{1,0:T(8,128)S(1)} %add_add_fusion.1), channel_id=1, source_target_pairs={{0,6},{1,7},{2,4},{3,5},{4,2},{5,3},{6,0},{7,1},{8,14},{9,15},{10,... | collective-permute-start | bytes 73736 | tf_op jit(solution)/shard_map/ppermute | solution.py:312
  36.8 4.2 %collective-permute-start.12 = (f32[48,128]{1,0:T(8,128)S(1)}, f32[48,128]{1,0:T(8,128)S(1)}, u32[]{:S(2)}, u32[]{:S(2)}) collective-permute-start(f32[48,128]{1,0:T(8,128)S(1)} %add_add_fusion.1), channel_id=1, source_target_pairs={{0,5},{1,4},{2,7},{3,6},{4,1},{5,0},{6,3},{7,2},{8,13},{9,12},{10,... | collective-permute-start | bytes 73736 | tf_op jit(solution)/shard_map/ppermute | solution.py:312
where the time goes:
time: 43.8 us; the launch traced here: 43.6 us
  starting transfers between devices  15.6 us (36%)
  Pallas kernels  14.1 us (32%)
  waiting for transfers between devices  13.2 us (30%)
  between operations  0.73 us (2%)
    ppermute x15, starting transfers between devices, permute(): lax.ppermute(values, ('sub', 'rep'), [(at, at ^ offset) for at in range(p...  15.6 us
    ppermute x15, waiting for transfers between devices, permute(): lax.ppermute(values, ('sub', 'rep'), [(at, at ^ offset) for at in range(p...  13.2 us
    pallas_call x1, Pallas kernels, fused_body(): call(ready_kernel, [(dual_ops.shape, dual_ops.dtype), matrix, tall, tall]...  4.56 us
    pallas_call x1, Pallas kernels, fused_body(): call(final_kernel, [((loads, rows), f32), ((MODES * groups, loads), f32)]...  2.6 us
    pallas_call x1, Pallas kernels, fused_body(): call(place_kernel, [((rows, rows + per_peer), jnp.bfloat16), ((loads + GR...  2.34 us
    pallas_call x1, Pallas kernels, fused_body(): call(second_kernel, [tall, wide], [VMEM] * (6 + len(got)), 'second')  1.87 us
    pallas_call x1, Pallas kernels, fused_body(): call(middle_kernel, [tall, tall, wide], [VMEM] * (4 + len(got)), 'middle'...  1.56 us
    pallas_call x1, Pallas kernels, fused_body(): call(first_kernel, [tall, *blocks(height)], [VMEM] * (3 + len(got)), 'fir...  1.11 us
  transfers between devices with their start and end apart: 15, of which 11 were waited for; matrix products, arithmetic and copies ran while one was open for 0% of the time, Pallas kernels for 14%

commit v1 on v0

--- a/solution.py
+++ b/solution.py
@@ -33,16 +33,21 @@
     return jnp.dot(left, right, precision=HIGHEST, preferred_element_type=jnp.float32)
 
 
-def send_blocks(values, place_ref, near_ref, own_ref, *pair_refs):
-    height, per_peer = own_ref.shape
-    peers = 2 * len(pair_refs) + 2
-    slots = split_dot(values, place_ref[:, : peers * per_peer], NN)
-    own_ref[...] = slots[:, :per_peer]
-    near_ref[...] = slots[:, per_peer : 2 * per_peer]
-    for at, ref in enumerate(pair_refs):
-        start = (peers - 2 * at - 2) * per_peer
+def send_far(values, far_ref, *pair_refs):
+    height = values.shape[0]
+    per_peer = pair_refs[0].shape[1]
+    slots = split_dot(values, far_ref[...], NN)
+    for at, ref in enumerate(reversed(pair_refs)):
+        start = 2 * at * per_peer
         ref[:height] = slots[:, start + per_peer : start + 2 * per_peer]
         ref[height:] = slots[:, start : start + per_peer]
+
+
+def send_near(values, place_ref, near_ref, own_ref):
+    per_peer = own_ref.shape[1]
+    slots = split_dot(values, place_ref[:, : 2 * per_peer], NN)
+    own_ref[...] = slots[:, :per_peer]
+    near_ref[...] = slots[:, per_peer:]
 
 
 def received(near_ref, own_ref, *pair_refs):
@@ -66,13 +71,19 @@
     return place_ref[:, place_ref.shape[1] - rows :]
 
 
+def one_hot(route_ref, peer, per_peer):
+    start = pl.multiple_of(peer * per_peer, per_peer)
+    row_ids = lax.broadcasted_iota(jnp.int32, (route_ref.shape[1], per_peer), 0)
+    return jnp.where(row_ids == route_ref[:, pl.ds(start, per_peer)], 1.0, 0.0).astype(jnp.bfloat16)
+
+
 def place_kernel(
-    route_hbm, block_hbm, gap_hbm, traces_hbm,
-    place_ref, values_ref, *refs,
+    route_hbm, block_hbm, gap_hbm, traces_hbm, operator_hbm,
+    far_ref, values_ref, operator_ref, route_ref, *refs,
 ):
-    *send_refs, route_ref, block_ref, traces_ref, sems = refs
+    *pair_refs, block_ref, traces_ref, sems = refs
     loads, rows = gap_hbm.shape
-    per_peer = send_refs[0].shape[1]
+    per_peer = pair_refs[0].shape[1]
     peers = rows // per_peer
     copies = [
         pltpu.make_async_copy(source, target, sems.at[at])
@@ -82,6 +93,7 @@
                 (block_hbm, block_ref),
                 (traces_hbm, traces_ref),
                 (gap_hbm, values_ref.at[pl.ds(0, loads)]),
+                (operator_hbm, operator_ref),
             )
         )
     ]
@@ -89,19 +101,10 @@
         copy.start()
     own_index = lax.axis_index("sub")
     device = own_index * lax.axis_size("rep") + lax.axis_index("rep")
-    row_ids = lax.broadcasted_iota(jnp.int32, (rows, per_peer), 0)
-    low = lax.broadcasted_iota(jnp.int32, (per_peer, per_peer), 0)
-    high = lax.broadcasted_iota(jnp.int32, (per_peer, per_peer), 1)
-    reverse = jnp.where(low + high == per_peer - 1, 1.0, 0.0).astype(jnp.bfloat16)
     copies[0].wait()
-    for offset in range(peers):
-        start = pl.multiple_of((own_index ^ offset) * per_peer, per_peer)
-        hits = row_ids == route_ref[:, pl.ds(start, per_peer)]
-        at = (offset if offset else peers) * per_peer
-        place_ref[:, at : at + per_peer] = jnp.where(hits, 1.0, 0.0).astype(jnp.bfloat16)
-    place_ref[:, :per_peer] = jnp.dot(
-        place_ref[:, rows:], reverse, preferred_element_type=jnp.float32
-    ).astype(jnp.bfloat16)
+    for offset in range(2, peers):
+        at = (offset - 2) * per_peer
+        far_ref[:, at : at + per_peer] = one_hot(route_ref, own_index ^ offset, per_peer)
     copies[1].wait()
     copies[2].wait()
     blocks = block_ref[...]
@@ -114,17 +117,30 @@
     values_ref[loads + modes : loads + modes + 1] = label
     values_ref[loads + modes + 1 :] = jnp.zeros((GROUP - modes - 1, rows), jnp.float32)
     copies[3].wait()
-    send_blocks(values_ref[...], place_ref, *send_refs)
-
-
-def ready_kernel(operator_hbm, place_ref, values_ref, operator_ref, placed_ref, own_ref, image_ref, sem):
-    copy = pltpu.make_async_copy(operator_hbm, operator_ref, sem)
-    copy.start()
+    send_far(values_ref[...], far_ref, *pair_refs)
+    copies[4].wait()
+
+
+def ready_kernel(
+    route_ref, far_ref, values_ref, operator_ref,
+    place_ref, placed_ref, own_ref, image_ref, near_ref, back_ref,
+):
+    rows = place_ref.shape[0]
+    per_peer = back_ref.shape[1]
+    own_index = lax.axis_index("sub")
+    low = lax.broadcasted_iota(jnp.int32, (per_peer, per_peer), 0)
+    high = lax.broadcasted_iota(jnp.int32, (per_peer, per_peer), 1)
+    reverse = jnp.where(low + high == per_peer - 1, 1.0, 0.0).astype(jnp.bfloat16)
+    own_columns = one_hot(route_ref, own_index, per_peer)
+    place_ref[:, rows:] = own_columns
+    place_ref[:, per_peer : 2 * per_peer] = one_hot(route_ref, own_index ^ 1, per_peer)
+    place_ref[:, 2 * per_peer : rows] = far_ref[...]
+    place_ref[:, :per_peer] = jnp.dot(own_columns, reverse, preferred_element_type=jnp.float32).astype(jnp.bfloat16)
     values = values_ref[...]
+    send_near(values, place_ref, near_ref, back_ref)
     loads = values.shape[0] - GROUP
     own = spread(values, loads, (own_ref.shape[0] - loads) // GROUP)
     own_ref[...] = own
-    copy.wait()
     operator = operator_ref[0]
     image_ref[...] = split_dot(own, operator, NT)
     placed_ref[...] = jnp.dot(
@@ -132,14 +148,14 @@
     ).astype(operator.dtype)
 
 
-def first_kernel(place_ref, placed_ref, own_image_ref, *refs):
-    half = len(refs) // 2
-    got_refs, (image_ref, *send_refs) = refs[:half], refs[half:]
+def first_kernel(far_ref, placed_ref, own_image_ref, *refs):
+    half = (len(refs) + 1) // 2
+    got_refs, (image_ref, *pair_refs) = refs[:half], refs[half:]
     height = got_refs[1].shape[0]
     got = spread(received(*got_refs), height - GROUP, (image_ref.shape[0] - height) // GROUP + 1)
     image = own_image_ref[...] - split_dot(got, placed_ref[...], NT)
     image_ref[...] = image
-    send_blocks(image, place_ref, *send_refs)
+    send_far(image, far_ref, *pair_refs)
 
 
 def products_of(left, right):
@@ -156,7 +172,8 @@
 
 
 def middle_kernel(place_ref, operator_ref, own_ref, image_ref, *refs):
-    *got_refs, basis_ref, twice_ref, terms_ref = refs
+    *got_refs, basis_ref, twice_ref, terms_ref, near_ref, back_ref = refs
+    send_near(image_ref[...], place_ref, near_ref, back_ref)
     coarse = terms_ref.shape[1] // 8
     loads = own_ref.shape[0] - coarse
     got = spread(received(*got_refs), loads, coarse // GROUP)
@@ -312,11 +329,13 @@
     return lax.ppermute(values, ("sub", "rep"), [(at, at ^ offset) for at in range(peers * planes)])
 
 
-def exchange(near, own, *pairs):
+def to_chips(*pairs):
+    return [permute(pair, 2 * (len(pairs) - at) + 1) for at, pair in enumerate(pairs)]
+
+
+def to_core(near, own, *pairs):
     height = own.shape[0]
-    pairs = [permute(pair, 2 * (len(pairs) - at) + 1) for at, pair in enumerate(pairs)]
-    near = permute(jnp.concatenate([near, *(pair[height:] for pair in pairs)], axis=0), 1)
-    return near, own, *pairs
+    return permute(jnp.concatenate([near, *(pair[height:] for pair in pairs)], axis=0), 1), own, *pairs
 
 
 def total(terms):
@@ -342,46 +361,52 @@
     tall = ((height, rows), f32)
     wide = ((height, 8 * GROUP * groups), f32)
 
-    def blocks(height):
-        return [((height, per_peer), f32)] * 2 + [((2 * height, per_peer), f32)] * (peers // 2 - 1)
+    def pairs(height):
+        return [((2 * height, per_peer), f32)] * (peers // 2 - 1)
+
+    def singles(height):
+        return [((height, per_peer), f32)] * 2
 
     def held(value):
         return pltpu.with_memory_space_constraint(value, pltpu.HBM)
 
     matrix = ((rows, rows), dual_ops.dtype)
-    inputs = [route, mode_block.reshape(1, subs), local_gap, mode_traces.transpose(1, 0, 2)]
-    place, values, *send = call(
+    inputs = [route, mode_block.reshape(1, subs), local_gap, mode_traces.transpose(1, 0, 2), dual_ops]
+    short = loads + GROUP
+    far, values, operator, route, *send = call(
         place_kernel,
-        [((rows, rows + per_peer), jnp.bfloat16), ((loads + GROUP, rows), f32), *blocks(loads + GROUP)],
-        [HBM] * 4,
+        [
+            ((rows, rows - 2 * per_peer), jnp.bfloat16),
+            ((short, rows), f32),
+            (dual_ops.shape, dual_ops.dtype),
+            (route.shape, i32),
+            *pairs(short),
+        ],
+        [HBM] * 5,
         "place",
-        [
-            pltpu.VMEM((1, rows), i32),
-            pltpu.VMEM((1, subs), i32),
-            pltpu.VMEM((modes, 1, rows), f32),
-            pltpu.SemaphoreType.DMA((4,)),
-        ],
+        [pltpu.VMEM((1, subs), i32), pltpu.VMEM((modes, 1, rows), f32), pltpu.SemaphoreType.DMA((5,))],
     )(*(held(value) for value in inputs))
-    got = exchange(*send)
-    operator, placed, own, own_image = call(
+    got = to_chips(*send)
+    place, placed, own, own_image, *stay = call(
         ready_kernel,
-        [(dual_ops.shape, dual_ops.dtype), matrix, tall, tall],
-        [HBM, VMEM, VMEM],
+        [((rows, rows + per_peer), jnp.bfloat16), matrix, tall, tall, *singles(short)],
+        [VMEM] * 4,
         "ready",
-        [pltpu.SemaphoreType.DMA],
-        2 * rows * rows * (rows + 2 * height),
-    )(held(dual_ops), place, values)
-    image, *send = call(first_kernel, [tall, *blocks(height)], [VMEM] * (3 + len(got)), "first")(
-        place, placed, own_image, *got
-    )
-    got_image = exchange(*send)
-    basis, twice, terms = call(
+        flops=2 * rows * rows * (rows + 2 * height),
+    )(route, far, values, operator)
+    got = to_core(*stay, *got)
+    image, *send = call(first_kernel, [tall, *pairs(height)], [VMEM] * (3 + len(got)), "first")(
+        far, placed, own_image, *got
+    )
+    got_image = to_chips(*send)
+    basis, twice, terms, *stay = call(
         middle_kernel,
-        [tall, tall, wide],
+        [tall, tall, wide, *singles(height)],
         [VMEM] * (4 + len(got)),
         "middle",
         flops=8 * rows * rows * height,
     )(place, operator, own, image, *got)
+    got_image = to_core(*stay, *got_image)
     jump, terms = call(second_kernel, [tall, wide], [VMEM] * (6 + len(got)), "second")(
         place, placed, basis, image, twice, terms, *got_image
     )

time: 43.8 us -> 39.7 us (0.906)
  waiting for transfers between devices: 13.2 us -> 10.8 us
  Pallas kernels: 14.1 us -> 12.4 us
    ppermute x15, waiting for transfers between devices: 13.2 us -> 10.8 us  [permute(): lax.ppermute(values, ('sub', 'rep'), [(at, at ^ offset) for at in range(p...]
    pallas_call x4, Pallas kernels: 9.58 us -> 7.88 us  [the longest x1 3.36 us: fused_body(): call(ready_kernel, [((rows, rows + per_peer), jnp.bfloat16), matrix, tall...]
  transfers between devices with their start and end apart: 15 -> 15, of which waited for: 11 -> 11; matrix products, arithmetic and copies ran while one was open for 0% -> 0% of each run, Pallas kernels for 14% -> 13%
where the time goes in v1:
time: 39.7 us; the launch traced here: 39.5 us
  starting transfers between devices  15.5 us (39%)
  Pallas kernels  12.4 us (31%)
  waiting for transfers between devices  10.8 us (27%)
  between operations  0.74 us (2%)
    ppermute x15, starting transfers between devices, permute(): lax.ppermute(values, ('sub', 'rep'), [(at, at ^ offset) for at in range(p...  15.5 us
    ppermute x15, waiting for transfers between devices, permute(): lax.ppermute(values, ('sub', 'rep'), [(at, at ^ offset) for at in range(p...  10.8 us
    pallas_call x1, Pallas kernels, fused_body(): call(ready_kernel, [((rows, rows + per_peer), jnp.bfloat16), matrix, tall...  3.36 us
    pallas_call x1, Pallas kernels, fused_body(): call(final_kernel, [((loads, rows), f32), ((MODES * groups, loads), f32)]...  2.6 us
    pallas_call x1, Pallas kernels, fused_body(): call(second_kernel, [tall, wide], [VMEM] * (6 + len(got)), 'second')  1.88 us
    pallas_call x1, Pallas kernels, fused_body(): call(place_kernel, [((rows, rows - 2 * per_peer), jnp.bfloat16), ((short,...  1.77 us
    pallas_call x1, Pallas kernels, fused_body(): call(middle_kernel, [tall, tall, wide, *singles(height)], [VMEM] * (4 + l...  1.64 us
    pallas_call x1, Pallas kernels, fused_body(): call(first_kernel, [tall, *pairs(height)], [VMEM] * (3 + len(got)), 'first')  1.12 us
  transfers between devices with their start and end apart: 15, of which 11 were waited for; matrix products, arithmetic and copies ran while one was open for 0% of the time, Pallas kernels for 13%

profile of v1, /device:TPU:0, one launch (start us, length us, event | category | flops | bytes accessed | tf_op | source)
XLA Modules:
  0.0 39.5 jit_solution(10407245084006975120)
XLA Ops:
  0.6 1.8 %place.1 = (bf16[1024,768]{1,0:T(8,128)(2,1)S(1)}, f32[40,1024]{1,0:T(8,128)S(1)}, bf16[1,1024,1024]{2,1,0:T(8,128)(2,1)S(1)}, s32[1,1024]{1,0:T(1,128)S(1)}, f3...) custom-call(s32[1,1024]{1,0:T(1,128)} %route_hbm.1, s32[1,32]{1,0:T(1,128)} %bitcast.4, ...), custom_call_target="tpu_custom_call" | custom-call | bytes 1048576 | tf_op jit(solution)/shard_map/place/pallas_call | solution.py:376
  2.4 3.4 %collective-permute-start = (f32[80,128]{1,0:T(8,128)S(1)}, f32[80,128]{1,0:T(8,128)S(1)}, u32[]{:S(2)}, u32[]{:S(2)}) collective-permute-start(f32[80,128]{1,0:T(8,128)S(1)} %get-tuple-element.37), channel_id=1, source_target_pairs={{0,28},{1,29},{2,30},{3,31},{4,24},{5,25},{6,26},{7,27},{8,20},{9,... | collective-permute-start | bytes 122888 | tf_op jit(solution)/shard_map/ppermute | solution.py:329
  5.8 0.8 %collective-permute-start.1 = (f32[80,128]{1,0:T(8,128)S(1)}, f32[80,128]{1,0:T(8,128)S(1)}, u32[]{:S(2)}, u32[]{:S(2)}) collective-permute-start(f32[80,128]{1,0:T(8,128)S(1)} %get-tuple-element.38), channel_id=1, source_target_pairs={{0,20},{1,21},{2,22},{3,23},{4,16},{5,17},{6,18},{7,19},{8,28},{9,... | collective-permute-start | bytes 122888 | tf_op jit(solution)/shard_map/ppermute | solution.py:329
  6.6 0.1 collective-permute-start.2
  6.7 3.4 %ready.1 = (bf16[1024,1152]{1,0:T(8,128)(2,1)S(1)}, bf16[1024,1024]{1,0:T(8,128)(2,1)S(1)}, f32[48,1024]{1,0:T(8,128)S(1)}, f32[48,1024]{1,0:T(8,128)S(1)}, f32[...) custom-call(s32[1,1024]{1,0:T(1,128)S(1)} %get-tuple-element.28.route_ref, bf16[1024,768]{1,0:T(8,128)(2,1)S(1)} %get-tuple-element.29.far_ref, ...), custom_call_target="tpu_custom_call" | custom-call | flops 2348810240 | bytes 1048576 | tf_op jit(solution)/shard_map/ready/pallas_call | solution.py:390
  10.1 0.0 collective-permute-done.refs_2_
  10.1 0.0 collective-permute-done.1.refs_3_
  10.1 0.2 collective-permute-done.2.refs_4_
  10.4 0.2 collective-permute-start.3
  10.6 1.2 %collective-permute-done.3.refs_0_ = f32[160,128]{1,0:T(8,128)S(1)} collective-permute-done((f32[160,128]{1,0:T(8,128)S(1)}, f32[160,128]{1,0:T(8,128)S(1)}, u32[]{:S(2)}, u32[]{:S(2)}) %collective-permute-start.3) | collective-permute-done | bytes 81952 | tf_op jit(solution)/shard_map/ppermute | solution.py:329
  11.7 1.1 %first.1 = (f32[48,1024]{1,0:T(8,128)S(1)}, f32[96,128]{1,0:T(8,128)S(1)}, f32[96,128]{1,0:T(8,128)S(1)}, f32[96,128]{1,0:T(8,128)S(1)}) custom-call(bf16[1024,768]{1,0:T(8,128)(2,1)S(1)} %get-tuple-element.29.far_ref, bf16[1024,1024]{1,0:T(8,128)(2,1)S(1)} %get-tuple-element.33.placed_ref, f32[48,1024]{1,0:T(8,128)S(1)} %get-tuple-element.35.own_image_ref, ...), custom_call_target="tpu_custom_call" | custom-call | bytes 1048576 | tf_op jit(solution)/shard_map/first/pallas_call | solution.py:398
  12.9 2.4 %collective-permute-start.4 = (f32[96,128]{1,0:T(8,128)S(1)}, f32[96,128]{1,0:T(8,128)S(1)}, u32[]{:S(2)}, u32[]{:S(2)}) collective-permute-start(f32[96,128]{1,0:T(8,128)S(1)} %get-tuple-element.46), channel_id=1, source_target_pairs={{0,28},{1,29},{2,30},{3,31},{4,24},{5,25},{6,26},{7,27},{8,20},{9,... | collective-permute-start | bytes 147464 | tf_op jit(solution)/shard_map/ppermute | solution.py:329
  15.2 0.3 collective-permute-start.5
  15.5 0.4 collective-permute-start.6
  15.8 1.6 %middle.1 = (f32[48,1024]{1,0:T(8,128)S(1)}, f32[48,1024]{1,0:T(8,128)S(1)}, f32[48,128]{1,0:T(8,128)S(1)}, f32[48,128]{1,0:T(8,128)S(1)}, f32[48,128]{1,0:T(8,128)S(1)}) custom-call(bf16[1024,1152]{1,0:T(8,128)(2,1)S(1)} %get-tuple-element.32.place_ref, bf16[1,1024,1024]{2,1,0:T(8,128)(2,1)S(1)} %get-tuple-element.31.operator_ref, ...), custom_call_target="tpu_custom_call" | custom-call | flops 402653184 | bytes 1048576 | tf_op jit(solution)/shard_map/middle/pallas_call | solution.py:402
  17.5 0.0 collective-permute-done.4.refs_2_
  17.5 1.4 %collective-permute-done.5.refs_3_ = f32[96,128]{1,0:T(8,128)S(1)} collective-permute-done((f32[96,128]{1,0:T(8,128)S(1)}, f32[96,128]{1,0:T(8,128)S(1)}, u32[]{:S(2)}, u32[]{:S(2)}) %collective-permute-start.5) | collective-permute-done | bytes 49184 | tf_op jit(solution)/shard_map/ppermute | solution.py:329
  18.9 0.1 collective-permute-done.6.refs_4_
  19.0 0.4 %collective-permute-start.7 = (f32[192,128]{1,0:T(8,128)S(1)}, f32[192,128]{1,0:T(8,128)S(1)}, u32[]{:S(2)}, u32[]{:S(2)}) collective-permute-start(f32[192,128]{1,0:T(8,128)S(1)} %pad_maximum_fusion), channel_id=1, source_target_pairs={{0,4},{1,5},{2,6},{3,7},{4,0},{5,1},{6,2},{7,3},{8,12},{9,13},{10,... | collective-permute-start | bytes 294920 | tf_op jit(solution)/shard_map/ppermute | solution.py:329
  19.4 0.9 %collective-permute-done.7.refs_0_ = f32[192,128]{1,0:T(8,128)S(1)} collective-permute-done((f32[192,128]{1,0:T(8,128)S(1)}, f32[192,128]{1,0:T(8,128)S(1)}, u32[]{:S(2)}, u32[]{:S(2)}) %collective-permute-start.7) | collective-permute-done | bytes 98336 | tf_op jit(solution)/shard_map/ppermute | solution.py:329
  20.4 1.9 %second.1 = (f32[48,1024]{1,0:T(8,128)S(1)}, f32[48,128]{1,0:T(8,128)S(1)}) custom-call(bf16[1024,1152]{1,0:T(8,128)(2,1)S(1)} %get-tuple-element.32.place_ref, bf16[1024,1024]{1,0:T(8,128)(2,1)S(1)} %get-tuple-element.33.placed_ref, f32[48,1024]{1,0:T(8,128)S(1)} %get-tuple-element.42.basis_ref, f32[48,1024]{1,0:T(8,128)S(1)} %get-tuple-element.41.image_ref, ...), custom_call_target="tpu_custom_call" | custom-call | bytes 1048576 | tf_op jit(solution)/shard_map/second/pallas_call | solution.py:410
  22.3 0.4 %collective-permute-start.8 = (f32[48,128]{1,0:T(8,128)S(1)}, f32[48,128]{1,0:T(8,128)S(1)}, u32[]{:S(2)}, u32[]{:S(2)}) collective-permute-start(f32[48,128]{1,0:T(8,128)S(1)} %get-tuple-element.50), channel_id=1, source_target_pairs={{0,4},{1,5},{2,6},{3,7},{4,0},{5,1},{6,2},{7,3},{8,12},{9,13},{10,... | collective-permute-start | bytes 73736 | tf_op jit(solution)/shard_map/ppermute | solution.py:329
  22.7 0.8 %collective-permute-done.8 = f32[48,128]{1,0:T(8,128)S(1)} collective-permute-done((f32[48,128]{1,0:T(8,128)S(1)}, f32[48,128]{1,0:T(8,128)S(1)}, u32[]{:S(2)}, u32[]{:S(2)}) %collective-permute-start.8) | collective-permute-done | bytes 24608 | tf_op jit(solution)/shard_map/ppermute | solution.py:329
  23.6 1.6 %collective-permute-start.11 = (f32[48,128]{1,0:T(8,128)S(1)}, f32[48,128]{1,0:T(8,128)S(1)}, u32[]{:S(2)}, u32[]{:S(2)}) collective-permute-start(f32[48,128]{1,0:T(8,128)S(1)} %add.21), channel_id=1, source_target_pairs={{0,28},{1,29},{2,30},{3,31},{4,24},{5,25},{6,26},{7,27},{8,20},{9,... | collective-permute-start | bytes 73736 | tf_op jit(solution)/shard_map/ppermute | solution.py:329
  25.1 0.9 %collective-permute-start.10 = (f32[48,128]{1,0:T(8,128)S(1)}, f32[48,128]{1,0:T(8,128)S(1)}, u32[]{:S(2)}, u32[]{:S(2)}) collective-permute-start(f32[48,128]{1,0:T(8,128)S(1)} %add.21), channel_id=1, source_target_pairs={{0,20},{1,21},{2,22},{3,23},{4,16},{5,17},{6,18},{7,19},{8,28},{9,... | collective-permute-start | bytes 73736 | tf_op jit(solution)/shard_map/ppermute | solution.py:329
  26.0 0.7 %collective-permute-start.9 = (f32[48,128]{1,0:T(8,128)S(1)}, f32[48,128]{1,0:T(8,128)S(1)}, u32[]{:S(2)}, u32[]{:S(2)}) collective-permute-start(f32[48,128]{1,0:T(8,128)S(1)} %add.21), channel_id=1, source_target_pairs={{0,12},{1,13},{2,14},{3,15},{4,8},{5,9},{6,10},{7,11},{8,4},{9,5},... | collective-permute-start | bytes 73736 | tf_op jit(solution)/shard_map/ppermute | solution.py:329
  26.7 1.0 %collective-permute-done.11 = f32[48,128]{1,0:T(8,128)S(1)} collective-permute-done((f32[48,128]{1,0:T(8,128)S(1)}, f32[48,128]{1,0:T(8,128)S(1)}, u32[]{:S(2)}, u32[]{:S(2)}) %collective-permute-start.11) | collective-permute-done | bytes 24608 | tf_op jit(solution)/shard_map/ppermute | solution.py:329
  27.7 0.8 %collective-permute-done.10 = f32[48,128]{1,0:T(8,128)S(1)} collective-permute-done((f32[48,128]{1,0:T(8,128)S(1)}, f32[48,128]{1,0:T(8,128)S(1)}, u32[]{:S(2)}, u32[]{:S(2)}) %collective-permute-start.10) | collective-permute-done | bytes 24608 | tf_op jit(solution)/shard_map/ppermute | solution.py:329
  28.5 0.8 %collective-permute-done.9 = f32[48,128]{1,0:T(8,128)S(1)} collective-permute-done((f32[48,128]{1,0:T(8,128)S(1)}, f32[48,128]{1,0:T(8,128)S(1)}, u32[]{:S(2)}, u32[]{:S(2)}) %collective-permute-start.9) | collective-permute-done | bytes 24608 | tf_op jit(solution)/shard_map/ppermute | solution.py:329
  29.3 3.4 %collective-permute-start.14 = (f32[48,128]{1,0:T(8,128)S(1)}, f32[48,128]{1,0:T(8,128)S(1)}, u32[]{:S(2)}, u32[]{:S(2)}) collective-permute-start(f32[48,128]{1,0:T(8,128)S(1)} %add_add_fusion.1), channel_id=1, source_target_pairs={{0,7},{1,6},{2,5},{3,4},{4,3},{5,2},{6,1},{7,0},{8,15},{9,14},{10,... | collective-permute-start | bytes 73736 | tf_op jit(solution)/shard_map/ppermute | solution.py:329
  32.7 0.0 collective-permute-start.13
  32.7 0.6 %collective-permute-start.12 = (f32[48,128]{1,0:T(8,128)S(1)}, f32[48,128]{1,0:T(8,128)S(1)}, u32[]{:S(2)}, u32[]{:S(2)}) collective-permute-start(f32[48,128]{1,0:T(8,128)S(1)} %add_add_fusion.1), channel_id=1, source_target_pairs={{0,5},{1,4},{2,7},{3,6},{4,1},{5,0},{6,3},{7,2},{8,13},{9,12},{10,... | collective-permute-start | bytes 73736 | tf_op jit(solution)/shard_map/ppermute | solution.py:329
  33.3 1.1 %collective-permute-done.14 = f32[48,128]{1,0:T(8,128)S(1)} collective-permute-done((f32[48,128]{1,0:T(8,128)S(1)}, f32[48,128]{1,0:T(8,128)S(1)}, u32[]{:S(2)}, u32[]{:S(2)}) %collective-permute-start.14) | collective-permute-done | bytes 24608 | tf_op jit(solution)/shard_map/ppermute | solution.py:329
  34.4 2.5 %collective-permute-done.13 = f32[48,128]{1,0:T(8,128)S(1)} collective-permute-done((f32[48,128]{1,0:T(8,128)S(1)}, f32[48,128]{1,0:T(8,128)S(1)}, u32[]{:S(2)}, u32[]{:S(2)}) %collective-permute-start.13) | collective-permute-done | bytes 24608 | tf_op jit(solution)/shard_map/ppermute | solution.py:329
  36.8 0.0 collective-permute-done.12
  36.9 2.6 %final.1 = (f32[32,1024]{1,0:T(8,128)}, f32[12,32]{1,0:T(8,128)}) custom-call(f32[48,128]{1,0:T(8,128)S(1)} %add_add_fusion.terms_ref, f32[48,1024]{1,0:T(8,128)S(1)} %get-tuple-element.42.basis_ref, f32[48,1024]{1,0:T(8,128)S(1)} %get-tuple-element.51.jump_ref), custom_call_target="tpu_custom_call" | custom-call | bytes 1048576 | tf_op jit(solution)/shard_map/final/pallas_call | solution.py:413
  (11 shorter events, 0.1 us)
Async XLA Ops:
  2.4 7.7 %collective-permute-start = (f32[80,128]{1,0:T(8,128)S(1)}, f32[80,128]{1,0:T(8,128)S(1)}, u32[]{:S(2)}, u32[]{:S(2)}) collective-permute-start(f32[80,128]{1,0:T(8,128)S(1)} %get-tuple-element.37), channel_id=1, source_target_pairs={{0,28},{1,29},{2,30},{3,31},{4,24},{5,25},{6,26},{7,27},{8,20},{9,... | collective-permute-start | bytes 122888 | tf_op jit(solution)/shard_map/ppermute | solution.py:329
  5.8 4.3 %collective-permute-start.1 = (f32[80,128]{1,0:T(8,128)S(1)}, f32[80,128]{1,0:T(8,128)S(1)}, u32[]{:S(2)}, u32[]{:S(2)}) collective-permute-start(f32[80,128]{1,0:T(8,128)S(1)} %get-tuple-element.38), channel_id=1, source_target_pairs={{0,20},{1,21},{2,22},{3,23},{4,16},{5,17},{6,18},{7,19},{8,28},{9,... | collective-permute-start | bytes 122888 | tf_op jit(solution)/shard_map/ppermute | solution.py:329
  6.6 3.8 %collective-permute-start.2 = (f32[80,128]{1,0:T(8,128)S(1)}, f32[80,128]{1,0:T(8,128)S(1)}, u32[]{:S(2)}, u32[]{:S(2)}) collective-permute-start(f32[80,128]{1,0:T(8,128)S(1)} %get-tuple-element.39), channel_id=1, source_target_pairs={{0,12},{1,13},{2,14},{3,15},{4,8},{5,9},{6,10},{7,11},{8,4},{9,5},... | collective-permute-start | bytes 122888 | tf_op jit(solution)/shard_map/ppermute | solution.py:329
  10.4 1.3 %collective-permute-start.3 = (f32[160,128]{1,0:T(8,128)S(1)}, f32[160,128]{1,0:T(8,128)S(1)}, u32[]{:S(2)}, u32[]{:S(2)}) collective-permute-start(f32[160,128]{1,0:T(8,128)S(1)} %pad_maximum_fusion.1), channel_id=1, source_target_pairs={{0,4},{1,5},{2,6},{3,7},{4,0},{5,1},{6,2},{7,3},{8,12},{9,13},{10,... | collective-permute-start | bytes 245768 | tf_op jit(solution)/shard_map/ppermute | solution.py:329
  12.9 4.6 %collective-permute-start.4 = (f32[96,128]{1,0:T(8,128)S(1)}, f32[96,128]{1,0:T(8,128)S(1)}, u32[]{:S(2)}, u32[]{:S(2)}) collective-permute-start(f32[96,128]{1,0:T(8,128)S(1)} %get-tuple-element.46), channel_id=1, source_target_pairs={{0,28},{1,29},{2,30},{3,31},{4,24},{5,25},{6,26},{7,27},{8,20},{9,... | collective-permute-start | bytes 147464 | tf_op jit(solution)/shard_map/ppermute | solution.py:329
  15.2 3.7 %collective-permute-start.5 = (f32[96,128]{1,0:T(8,128)S(1)}, f32[96,128]{1,0:T(8,128)S(1)}, u32[]{:S(2)}, u32[]{:S(2)}) collective-permute-start(f32[96,128]{1,0:T(8,128)S(1)} %get-tuple-element.47), channel_id=1, source_target_pairs={{0,20},{1,21},{2,22},{3,23},{4,16},{5,17},{6,18},{7,19},{8,28},{9,... | collective-permute-start | bytes 147464 | tf_op jit(solution)/shard_map/ppermute | solution.py:329
  15.5 3.5 %collective-permute-start.6 = (f32[96,128]{1,0:T(8,128)S(1)}, f32[96,128]{1,0:T(8,128)S(1)}, u32[]{:S(2)}, u32[]{:S(2)}) collective-permute-start(f32[96,128]{1,0:T(8,128)S(1)} %get-tuple-element.48), channel_id=1, source_target_pairs={{0,12},{1,13},{2,14},{3,15},{4,8},{5,9},{6,10},{7,11},{8,4},{9,5},... | collective-permute-start | bytes 147464 | tf_op jit(solution)/shard_map/ppermute | solution.py:329
  19.0 1.4 %collective-permute-start.7 = (f32[192,128]{1,0:T(8,128)S(1)}, f32[192,128]{1,0:T(8,128)S(1)}, u32[]{:S(2)}, u32[]{:S(2)}) collective-permute-start(f32[192,128]{1,0:T(8,128)S(1)} %pad_maximum_fusion), channel_id=1, source_target_pairs={{0,4},{1,5},{2,6},{3,7},{4,0},{5,1},{6,2},{7,3},{8,12},{9,13},{10,... | collective-permute-start | bytes 294920 | tf_op jit(solution)/shard_map/ppermute | solution.py:329
  22.3 1.3 %collective-permute-start.8 = (f32[48,128]{1,0:T(8,128)S(1)}, f32[48,128]{1,0:T(8,128)S(1)}, u32[]{:S(2)}, u32[]{:S(2)}) collective-permute-start(f32[48,128]{1,0:T(8,128)S(1)} %get-tuple-element.50), channel_id=1, source_target_pairs={{0,4},{1,5},{2,6},{3,7},{4,0},{5,1},{6,2},{7,3},{8,12},{9,13},{10,... | collective-permute-start | bytes 73736 | tf_op jit(solution)/shard_map/ppermute | solution.py:329
  23.6 4.2 %collective-permute-start.11 = (f32[48,128]{1,0:T(8,128)S(1)}, f32[48,128]{1,0:T(8,128)S(1)}, u32[]{:S(2)}, u32[]{:S(2)}) collective-permute-start(f32[48,128]{1,0:T(8,128)S(1)} %add.21), channel_id=1, source_target_pairs={{0,28},{1,29},{2,30},{3,31},{4,24},{5,25},{6,26},{7,27},{8,20},{9,... | collective-permute-start | bytes 73736 | tf_op jit(solution)/shard_map/ppermute | solution.py:329
  25.1 3.4 %collective-permute-start.10 = (f32[48,128]{1,0:T(8,128)S(1)}, f32[48,128]{1,0:T(8,128)S(1)}, u32[]{:S(2)}, u32[]{:S(2)}) collective-permute-start(f32[48,128]{1,0:T(8,128)S(1)} %add.21), channel_id=1, source_target_pairs={{0,20},{1,21},{2,22},{3,23},{4,16},{5,17},{6,18},{7,19},{8,28},{9,... | collective-permute-start | bytes 73736 | tf_op jit(solution)/shard_map/ppermute | solution.py:329
  26.0 3.3 %collective-permute-start.9 = (f32[48,128]{1,0:T(8,128)S(1)}, f32[48,128]{1,0:T(8,128)S(1)}, u32[]{:S(2)}, u32[]{:S(2)}) collective-permute-start(f32[48,128]{1,0:T(8,128)S(1)} %add.21), channel_id=1, source_target_pairs={{0,12},{1,13},{2,14},{3,15},{4,8},{5,9},{6,10},{7,11},{8,4},{9,5},... | collective-permute-start | bytes 73736 | tf_op jit(solution)/shard_map/ppermute | solution.py:329
  29.3 5.1 %collective-permute-start.14 = (f32[48,128]{1,0:T(8,128)S(1)}, f32[48,128]{1,0:T(8,128)S(1)}, u32[]{:S(2)}, u32[]{:S(2)}) collective-permute-start(f32[48,128]{1,0:T(8,128)S(1)} %add_add_fusion.1), channel_id=1, source_target_pairs={{0,7},{1,6},{2,5},{3,4},{4,3},{5,2},{6,1},{7,0},{8,15},{9,14},{10,... | collective-permute-start | bytes 73736 | tf_op jit(solution)/shard_map/ppermute | solution.py:329
  32.7 4.2 %collective-permute-start.13 = (f32[48,128]{1,0:T(8,128)S(1)}, f32[48,128]{1,0:T(8,128)S(1)}, u32[]{:S(2)}, u32[]{:S(2)}) collective-permute-start(f32[48,128]{1,0:T(8,128)S(1)} %add_add_fusion.1), channel_id=1, source_target_pairs={{0,6},{1,7},{2,4},{3,5},{4,2},{5,3},{6,0},{7,1},{8,14},{9,15},{10,... | collective-permute-start | bytes 73736 | tf_op jit(solution)/shard_map/ppermute | solution.py:329
  32.7 4.2 %collective-permute-start.12 = (f32[48,128]{1,0:T(8,128)S(1)}, f32[48,128]{1,0:T(8,128)S(1)}, u32[]{:S(2)}, u32[]{:S(2)}) collective-permute-start(f32[48,128]{1,0:T(8,128)S(1)} %add_add_fusion.1), channel_id=1, source_target_pairs={{0,5},{1,4},{2,7},{3,6},{4,1},{5,0},{6,3},{7,2},{8,13},{9,12},{10,... | collective-permute-start | bytes 73736 | tf_op jit(solution)/shard_map/ppermute | solution.py:329
